TPU v7x, 32 devices: a whole 2x2x4 slice. The times are simulated.
32 devices in a mesh: dp: 8 (over y, x, core), col: 4 (over z).
Axes of the slice: x: 2, y: 2, z: 4, core: 2. Of those that a mesh axis runs over, the one named last changes fastest.
Arguments:
- grad_out: bfloat16 [2048, 3584], P('dp', 'col'), may hold values from -6 to 6
- residual: bfloat16 [2048, 3584], P('dp', 'col'), may hold values from -6 to 6
- confounders: bfloat16 [2048, 512], P('dp'), may hold values from -6 to 6
- gram_factor: float32 [512, 512], replicated, as said below
- proj_weight: bfloat16 [3584, 3584], P('dp', 'col'), may hold values from -0.09375 to 0.09375
- doc_lengths: int32 [2048], P(('dp', 'col')), may hold values from 1 to 512, as said below
Outputs:
- token_grad: float32 [2048, 3584], P(('dp', 'col'))
- weight_grad: float32 [3584, 3584], P('dp', 'col')
Inputs may be any that keep to these rules, and one draw needn't show every extreme that they name: `gram_factor`: lower triangular with a positive diagonal. `doc_lengths`: at least one document has 512 tokens.
All inputs are finite; a program needn't handle non-finite values.
Results may differ from a plain program's by a relative error of at most 0.0026.
Values may be sent and summed in bfloat16 or wider, within the bound.
A program may use at most 64 MiB of HBM per device.

v0:
```python
import jax
import jax.numpy as jnp
from jax import lax
from jax.sharding import PartitionSpec as P


def solve_gram(factor, rhs):
    inner = lax.linalg.triangular_solve(factor, rhs, left_side=True, lower=True)
    return lax.linalg.triangular_solve(factor, inner, left_side=True, lower=True, transpose_a=True)


def shards(grad_out, residual, confounders, gram_factor, proj_weight, doc_lengths):
    grad_full = lax.all_gather(grad_out, "col", axis=1, tiled=True)
    docs_total = grad_out.shape[0] * lax.axis_size("dp")
    norm_scale = docs_total ** (-0.5)
    grad_block = grad_full
    summed = lax.psum_scatter(
        lax.dot_general(
            grad_block, residual, (((0,), (0,)), ((), ())), preferred_element_type=jnp.float32
        ),
        "dp",
        scatter_dimension=0,
        tiled=True,
    )
    weight_grad = summed * norm_scale
    grad_block = grad_full
    dense_grad = jnp.dot(
        grad_block,
        lax.all_gather(proj_weight, "dp", axis=0, tiled=True),
        preferred_element_type=jnp.float32,
    )
    dense_b = dense_grad.astype(jnp.bfloat16)
    partial_value = lax.dot_general(
        confounders, dense_b, (((0,), (0,)), ((), ())), preferred_element_type=jnp.float32
    )
    moments = lax.psum(partial_value, "dp")
    coef_b = solve_gram(gram_factor, moments).astype(jnp.bfloat16)
    pooled = dense_grad - jnp.dot(confounders, coef_b, preferred_element_type=jnp.float32)
    doc_grad = lax.all_to_all(pooled, "col", split_axis=0, concat_axis=1, tiled=True)
    token_grad = doc_grad / doc_lengths.astype(jnp.float32)[:, None]
    return (token_grad, weight_grad)


def solution(mesh):
    placed = (P("dp", "col"), P("dp", "col"), P("dp", None), P(), P("dp", "col"), P(("dp", "col")))
    return jax.shard_map(
        shards,
        mesh=mesh,
        in_specs=placed,
        out_specs=(P(("dp", "col"), None), P("dp", "col")),
        check_vma=False,
    )
```

profile of v0, /device:TPU:0, one launch (start us, length us, event | category | flops | bytes accessed | tf_op | source)
XLA Modules:
  0.0 274.9 jit_solution(5146423763550622942)
XLA Ops:
  8.7 45.1 %all-gather.3.cloned.1.call-done = bf16[256,3584]{1,0:T(8,128)(2,1)} async-done(((bf16[256,896]{1,0:T(8,128)(2,1)}), bf16[256,3584]{1,0:T(8,128)(2,1)}) %all-gather.3.cloned.1.call-update) | async-done | bytes 1835024 | tf_op jit(solution)/shard_map/all_gather | solution.py:13
  53.9 46.8 %all-gather.5.cloned.1.call-done = bf16[3584,896]{1,0:T(8,128)(2,1)} async-done(((bf16[448,896]{1,0:T(8,128)(2,1)}), bf16[3584,896]{1,0:T(8,128)(2,1)}) %all-gather.5.cloned.1.call-update) | async-done | bytes 6422544 | tf_op jit(solution)/shard_map/all_gather | solution.py:29
  100.7 5.4 %fusion.57 = f32[256,896]{1,0:T(8,128)S(1)} fusion(bf16[256,3584]{1,0:T(8,128)(2,1)} %all-gather.3.cloned.1.call-done, bf16[3584,896]{1,0:T(8,128)(2,1)} %all-gather.5.cloned.1.call-done), kind=kOutput, calls=%fused_computation.70 | convolution fusion | flops 1644167168 | bytes 9175040 | tf_op jit(solution)/shard_map/dot_general | solution.py:27
  106.2 1.7 convolution_bitcast_fusion
  107.9 6.7 %fusion.58 = f32[3584,896]{1,0:T(8,128)} fusion(bf16[256,3584]{1,0:T(8,128)(2,1)S(1)} %copy-done.1, bf16[256,896]{1,0:T(8,128)(2,1)S(1)} %copy-done), kind=kOutput, calls=%fused_computation.71 | convolution fusion | flops 1644167168 | bytes 15138816 | tf_op jit(solution)/shard_map/dot_general | solution.py:18
  114.7 1.2 copy-done.3
  116.0 10.7 %while.1 = (s32[]{:T(128)}, f32[512,512]{1,0:T(8,128)S(1)}, s32[4,2]{0,1:T(2,128)S(1)}, f32[4,128,128]{2,1,0:T(8,128)}, s32[]{:T(128)}) while((s32[]{:T(128)}, f32[512,512]{1,0:T(8,128)S(1)}, s32[4,2]{0,1:T(2,128)S(1)}, f32[4,128,128]{2,1,0:T(8,128)}, s32[]{:T(128)}) %tuple.26), condition=%wide.while_cond, body=%wide.while_body.sunk | while | flops 2 | bytes 132205 | solution.py:9
  116.6 2.0 bitcast_dynamic-update-slice_fusion.2
  119.3 2.0 bitcast_dynamic-update-slice_fusion.2
  122.0 2.0 bitcast_dynamic-update-slice_fusion.2
  124.7 2.0 bitcast_dynamic-update-slice_fusion.2
  126.7 40.3 %custom-call.5 = f32[4,128,128]{1,2,0:T(8,128)S(1)} custom-call(f32[4,128,128]{2,1,0:T(8,128)} %get-tuple-element.9), custom_call_target="InvertDiagBlocksLowerTriangular" | custom-call | tf_op jit(solution)/shard_map/triangular_solve | solution.py:9
  167.0 1.6 all-reduce.2.cloned.1.call-done
  168.6 1.8 fusion.33
  170.4 1.9 convolution_subtract_fusion.3
  172.9 1.6 convolution_subtract_fusion.1
  175.2 2.4 fusion.16
  181.0 1.1 fusion.13
  182.7 1.4 fusion.12
  184.0 4.9 %all-to-all-start = ((f32[4,64,896]{2,1,0:T(8,128)}), f32[4,64,896]{2,1,0:T(8,128)S(1)}, u32[]{:S(2)}, u32[]{:S(2)}) async-start(f32[4,64,896]{2,1,0:T(8,128)} %bitcast.6), calls=%async_computation | async-start | bytes 1835008 | tf_op jit(solution)/shard_map/all_to_all | solution.py:39
  189.0 21.8 %all-to-all-done = f32[4,64,896]{2,1,0:T(8,128)S(1)} async-done(((f32[4,64,896]{2,1,0:T(8,128)}), f32[4,64,896]{2,1,0:T(8,128)S(1)}, u32[]{:S(2)}, u32[]{:S(2)}) %all-to-all-start) | async-done | bytes 917536 | tf_op jit(solution)/shard_map/all_to_all | solution.py:39
  210.8 1.1 broadcast_divide_fusion
  211.9 53.7 %reduce-scatter.2.cloned.1.call-done = f32[448,896]{1,0:T(8,128)} async-done(((f32[3584,896]{1,0:T(8,128)}), f32[448,896]{1,0:T(8,128)}) %reduce-scatter.2.cloned.1.call-update) | async-done | bytes 1605648 | tf_op jit(solution)/shard_map/reduce_scatter | solution.py:17
  265.6 2.7 broadcast_multiply_fusion
  (44 shorter events, 9.6 us)
Async XLA Ops:
  7.2 100.7 %copy-start = (bf16[256,896]{1,0:T(8,128)(2,1)S(1)}, bf16[256,896]{1,0:T(8,128)(2,1)}, u32[]{:S(2)}) copy-start(bf16[256,896]{1,0:T(8,128)(2,1)} %param.7) | copy-start | bytes 1376260
  7.2 46.7 %all-gather.3.cloned.1.call-start = ((), (), s32[]{:S(2)}) async-start(), calls=%async_computation.2 | async-start | bytes 2293760 | tf_op jit(solution)/shard_map/all_gather | solution.py:13
  7.9 92.8 %all-gather.5.cloned.1.call-start = ((), (), s32[]{:S(2)}) async-start(), calls=%async_computation.3 | async-start | bytes 7225344 | tf_op jit(solution)/shard_map/all_gather | solution.py:29
  8.7 97.5 %copy-start.4 = (bf16[256,512]{1,0:T(8,128)(2,1)S(1)}, bf16[256,512]{1,0:T(8,128)(2,1)}, u32[]{:S(2)}) copy-start(bf16[256,512]{1,0:T(8,128)(2,1)} %param.8) | copy-start | bytes 786436
  8.7 159.9 %all-reduce.2.cloned.1.call-start = ((), (), s32[]{:S(2)}) async-start(), calls=%async_computation.4 | async-start | bytes 3670016 | tf_op jit(solution)/shard_map/psum | solution.py:36
  106.1 1.8 copy-start.1
  107.8 157.8 %reduce-scatter.2.cloned.1.call-start = ((), (), s32[]{:S(2)}) async-start(), calls=%async_computation.5 | async-start | bytes 14450688 | tf_op jit(solution)/shard_map/reduce_scatter | solution.py:17
  114.6 1.2 copy-start.3
  168.6 4.3 %copy-start.2 = (f32[512,896]{0,1:T(8,128)S(1)}, f32[512,896]{0,1:T(8,128)}, u32[]{:S(2)}) copy-start(f32[512,896]{0,1:T(8,128)} %all-reduce.2.cloned.1.call-done) | copy-start | bytes 5505028
  181.0 1.6 copy-start.5
  184.0 4.9 %copy-start.6 = (s32[64]{0:T(128)S(1)}, s32[64]{0:T(128)}, u32[]{:S(2)}) copy-start(s32[64]{0:T(128)} %param.11) | copy-start | bytes 772
  184.0 26.7 %all-to-all-start = ((f32[4,64,896]{2,1,0:T(8,128)}), f32[4,64,896]{2,1,0:T(8,128)S(1)}, u32[]{:S(2)}, u32[]{:S(2)}) async-start(f32[4,64,896]{2,1,0:T(8,128)} %bitcast.6), calls=%async_computation | async-start | bytes 1835008 | tf_op jit(solution)/shard_map/all_to_all | solution.py:39
Sparse Core Ops, SparseCore 0:
  9.6 44.2 all-gather.2
  55.7 44.8 all-gather.4
  108.0 60.5 all-reduce.1
  172.4 93.1 reduce-scatter.1
where the time goes:
time: 275 us
  waiting for transfers between devices  170 us (62%)
  other arithmetic  44.2 us (16%)
  matrix products  29.1 us (11%)
  between operations  14 us (5%)
  local copies, waits for them, and re-layouts  12 us (4%)
  starting transfers between devices  5.08 us (2%)
    reduce_scatter x1, waiting for transfers between devices, shards(): lax.psum_scatter(lax.dot_general(grad_block, residual, (((0,), (0,)), (()...  53.7 us
    all_gather x1, waiting for transfers between devices, shards(): lax.all_gather(proj_weight, 'dp', axis=0, tiled=True)  46.8 us
    all_gather x1, waiting for transfers between devices, shards(): grad_full = lax.all_gather(grad_out, 'col', axis=1, tiled=True)  45.1 us
    another operation x3, other arithmetic, solve_gram(): lax.linalg.triangular_solve(factor, inner, left_side=True, lower=True, tr...  40.4 us
    all_to_all x1, waiting for transfers between devices, shards(): lax.all_to_all(pooled, 'col', split_axis=0, concat_axis=1, tiled=True)  21.8 us
    another operation x12, local copies, waits for them, and re-layouts  10.7 us
    another operation x7, matrix products, solve_gram(): inner = lax.linalg.triangular_solve(factor, rhs, left_side=True, lower=True)  9.51 us
    dot_general x1, matrix products, shards(): lax.dot_general(grad_block, residual, (((0,), (0,)), ((), ())), preferred...  6.7 us
  transfers between devices with their start and end apart: 5, of which 5 were waited for; matrix products, arithmetic and copies ran while one was open for 27% of the time, Pallas kernels for 0%

commit v1 on v0

--- a/solution.py
+++ b/solution.py
@@ -1,6 +1,10 @@
+import functools
+
 import jax
 import jax.numpy as jnp
 from jax import lax
+from jax.experimental import pallas as pl
+from jax.experimental.pallas import tpu as pltpu
 from jax.sharding import PartitionSpec as P
 
 
@@ -41,10 +45,297 @@
     return (token_grad, weight_grad)
 
 
+F32, BF16 = jnp.float32, jnp.bfloat16
+EXACT = lax.Precision.HIGHEST
+
+
+def dot(a, b, da=1, db=0, precision=None):
+    return lax.dot_general(
+        a, b, (((da,), (db,)), ((), ())), preferred_element_type=F32, precision=precision
+    )
+
+
+def exact(a, b, da=1, db=0):
+    return dot(a, b, da, db, EXACT)
+
+
+def invert_factor(l_ref, inv_ref):
+    k, base = l_ref.shape[0], 128
+    r = lax.broadcasted_iota(jnp.int32, (base, base), 0)
+    c = lax.broadcasted_iota(jnp.int32, (base, base), 1)
+    diag = r == c
+    inv_ref[...] = jnp.zeros_like(inv_ref)
+    blocks = [l_ref[o : o + base, o : o + base] for o in range(0, k, base)]
+    parts = [jnp.where(diag, 1.0 / jnp.where(diag, b, 1.0), 0.0) for b in blocks]
+    size = 1
+    while size < base:
+        low = (r // (2 * size) == c // (2 * size)) & (r // size > c // size)
+        inner = [exact(jnp.where(low, b, 0.0), x) for b, x in zip(blocks, parts)]
+        parts = [x - exact(x, t) for x, t in zip(parts, inner)]
+        size *= 2
+    for at, x in enumerate(parts):
+        o = at * base
+        inv_ref[o : o + base, o : o + base] = x
+    while size < k:
+        for o in range(0, k, 2 * size):
+            mid, end = o + size, o + 2 * size
+            t = exact(l_ref[mid:end, o:mid], inv_ref[o:mid, o:mid])
+            inv_ref[mid:end, o:mid] = -exact(inv_ref[mid:end, mid:end], t)
+        size *= 2
+
+
+def kernel(
+    n, m, scale,
+    gt_ref, res_ref, conf_ref, fac_ref, w_ref, len_ref,
+    tok_ref, dw_ref,
+    gf, wf, rf, gx, r32, rb, mt, msib, mpre, mrecv, inv, cf, pb, prow, own,
+    g_s, g_r, w_s, w_r, r_s, r_r, x_s, x_r, a_s, a_r, m_s, m_r, c_s, c_r, p_s, p_r,
+):
+    dp, col = lax.axis_index("dp"), lax.axis_index("col")
+    core, chip = dp % 2, dp // 2
+    sib = dp + 1 - 2 * core
+    chips = n // 2
+    width, docs = gt_ref.shape
+    units = w_ref.shape[0]
+    share = docs // m
+    rows = width // n
+
+    def to_dp(src, dst, s, r, d):
+        return pltpu.make_async_remote_copy(
+            src, dst, s, r, device_id={"dp": d}, device_id_type=pl.DeviceIdType.MESH
+        )
+
+    def to_col(src, dst, s, r, d):
+        return pltpu.make_async_remote_copy(
+            src, dst, s, r, device_id={"col": d}, device_id_type=pl.DeviceIdType.MESH
+        )
+
+    def same_core(step):
+        return lax.rem(chip + step, chips) * 2 + core
+
+    def slot_of(t):
+        back = lax.rem(t, chips)
+        at = lax.rem(chip + chips - back, chips) * 2
+        return at + lax.rem(core + t // chips, 2)
+
+    def gather_start(ref, full, ss, rr):
+        copies = [
+            to_dp(ref, full.at[dp], ss.at[k], rr.at[k], same_core(k)) for k in range(1, chips)
+        ]
+        copies.append(to_dp(ref, full.at[dp], ss.at[chips], rr.at[chips], sib))
+        for copy in copies:
+            copy.start()
+        full[dp] = ref[...]
+
+    def gather_wait(full, ss, rr, t):
+        at = full.at[slot_of(t)]
+        to_dp(at, at, ss.at[t], rr.at[t], sib).wait_recv()
+
+    def gather_pass(full, ss, rr, t):
+        at = full.at[slot_of(t)]
+        to_dp(at, at, ss.at[chips + t], rr.at[chips + t], sib).start()
+
+    def gather_end(ref, full, ss, rr):
+        for t in range(1, n):
+            to_dp(ref, full.at[dp], ss.at[t], rr.at[t], sib).wait_send()
+
+    barrier = pltpu.get_barrier_semaphore()
+    for k in range(1, n):
+        pl.semaphore_signal(
+            barrier, inc=1, device_id={"dp": lax.rem(dp + k, n)}, device_id_type=pl.DeviceIdType.MESH
+        )
+    for k in range(1, m):
+        pl.semaphore_signal(
+            barrier, inc=1, device_id={"col": lax.rem(col + k, m)}, device_id_type=pl.DeviceIdType.MESH
+        )
+    pl.semaphore_wait(barrier, n + m - 2)
+
+    mine = pl.ds(pl.multiple_of(col * width, width), width)
+    g_copies = [
+        to_col(gt_ref, gf.at[mine], g_s.at[k], g_r.at[k], lax.rem(col + k, m)) for k in range(1, m)
+    ]
+    for copy in g_copies:
+        copy.start()
+    gather_start(w_ref, wf, w_s, w_r)
+    gf[mine, :] = gt_ref[...]
+
+    invert_factor(fac_ref, inv)
+
+    for copy in g_copies:
+        copy.wait_recv()
+
+    def add_units(t, first=False):
+        at = slot_of(t)
+        piece = gf[pl.ds(pl.multiple_of(at * units, units), units), :]
+        part = dot(piece, wf[at], 0, 0)
+        r32[...] = part if first else r32[...] + part
+
+    add_units(0, True)
+
+    @pl.loop(1, chips)
+    def _(t):
+        gather_wait(wf, w_s, w_r, t)
+        gather_pass(wf, w_s, w_r, t)
+        add_units(t)
+
+    @pl.loop(chips, n)
+    def _(t):
+        gather_wait(wf, w_s, w_r, t)
+        add_units(t)
+
+    rb[...] = r32[...].astype(BF16)
+    mt[...] = dot(rb[...], conf_ref[...], 0, 0)
+
+    a_copies = []
+    for q in range(chips):
+        there = pl.ds(pl.multiple_of((2 * q + 1 - core) * rows, rows), rows)
+        a_copies.append(to_dp(mt.at[there], msib.at[q], a_s.at[q], a_r.at[q], sib))
+    for copy in a_copies:
+        copy.start()
+    for copy in a_copies:
+        copy.wait_recv()
+    for q in range(chips):
+        here = pl.ds(pl.multiple_of((2 * q + core) * rows, rows), rows)
+        mpre[q] = mt[here, :] + msib[q]
+    m_copies = []
+    for k in range(1, chips):
+        q = lax.rem(chip + k, chips)
+        m_copies.append(to_dp(mpre.at[q], mrecv.at[k], m_s.at[k], m_r.at[k], same_core(k)))
+    for copy in m_copies:
+        copy.start()
+
+    gather_start(res_ref, rf, r_s, r_r)
+    x_copies = []
+    for k in range(1, n):
+        d = lax.rem(dp + k, n)
+        piece = gf.at[pl.ds(pl.multiple_of(d * units, units), units)]
+        x_copies.append(to_dp(piece, gx.at[dp], x_s.at[k], x_r.at[k], d))
+    for copy in x_copies:
+        copy.start()
+    gx[dp] = gf[pl.ds(pl.multiple_of(dp * units, units), units), :]
+
+    for copy in m_copies:
+        copy.wait_recv()
+    total = mpre[chip]
+    for k in range(1, chips):
+        total = total + mrecv[k]
+    coef = exact(exact(total, inv[...], 1, 1), inv[...])
+    own[...] = coef.astype(BF16)
+    gather_start(own, cf, c_s, c_r)
+
+    @pl.loop(1, chips)
+    def _(t):
+        gather_wait(cf, c_s, c_r, t)
+        gather_pass(cf, c_s, c_r, t)
+
+    @pl.loop(chips, n)
+    def _(t):
+        gather_wait(cf, c_s, c_r, t)
+
+    coef_all = cf[...].reshape(width, cf.shape[2])
+    r32[...] = r32[...] - dot(conf_ref[...], coef_all, 1, 1)
+    pb[...] = r32[...].astype(BF16)
+    p_copies = []
+    for k in range(1, m):
+        c = lax.rem(col + k, m)
+        piece = pb.at[pl.ds(pl.multiple_of(c * share, share), share)]
+        p_copies.append(to_col(piece, prow.at[col], p_s.at[k], p_r.at[k], c))
+    for copy in p_copies:
+        copy.start()
+
+    def add_docs(t, first=False):
+        at = slot_of(t)
+        part = dot(gx[at], rf[at]) * scale
+        dw_ref[...] = part if first else dw_ref[...] + part
+
+    @pl.loop(1, chips)
+    def _(t):
+        gather_wait(rf, r_s, r_r, t)
+        gather_pass(rf, r_s, r_r, t)
+
+    add_docs(0, True)
+    for copy in x_copies:
+        copy.wait_recv()
+
+    @pl.loop(1, chips)
+    def _(t):
+        add_docs(t)
+
+    @pl.loop(chips, n)
+    def _(t):
+        gather_wait(rf, r_s, r_r, t)
+        add_docs(t)
+
+    for copy in p_copies:
+        copy.wait_recv()
+    prow[col] = pb[pl.ds(pl.multiple_of(col * share, share), share), :]
+    for c in range(m):
+        tok_ref[:, c * width : (c + 1) * width] = prow[c].astype(F32) / len_ref[...]
+
+    gather_end(w_ref, wf, w_s, w_r)
+    gather_end(res_ref, rf, r_s, r_r)
+    gather_end(own, cf, c_s, c_r)
+    for copy in g_copies + a_copies + m_copies + x_copies + p_copies:
+        copy.wait_send()
+
+
+def fused(n, m, grad_out, residual, confounders, gram_factor, proj_weight, doc_lengths):
+    docs, width = grad_out.shape
+    units, k = proj_weight.shape[0], confounders.shape[1]
+    share, rows, chips = docs // m, width // n, n // 2
+    sem = pltpu.SemaphoreType.DMA
+    vmem = pl.BlockSpec(memory_space=pltpu.VMEM)
+    return pl.pallas_call(
+        functools.partial(kernel, n, m, (docs * n) ** (-0.5)),
+        out_shape=(
+            jax.ShapeDtypeStruct((share, width * m), F32),
+            jax.ShapeDtypeStruct((units, width), F32),
+        ),
+        in_specs=[vmem] * 6,
+        out_specs=(vmem, vmem),
+        scratch_shapes=[
+            pltpu.VMEM((width * m, docs), BF16),
+            pltpu.VMEM((n, units, width), BF16),
+            pltpu.VMEM((n, docs, width), BF16),
+            pltpu.VMEM((n, units, docs), BF16),
+            pltpu.VMEM((docs, width), F32),
+            pltpu.VMEM((docs, width), BF16),
+            pltpu.VMEM((width, k), F32),
+            pltpu.VMEM((chips, rows, k), F32),
+            pltpu.VMEM((chips, rows, k), F32),
+            pltpu.VMEM((chips, rows, k), F32),
+            pltpu.VMEM((k, k), F32),
+            pltpu.VMEM((n, rows, k), BF16),
+            pltpu.VMEM((docs, width), BF16),
+            pltpu.VMEM((m, share, width), BF16),
+            pltpu.VMEM((rows, k), BF16),
+        ]
+        + [sem((m,))] * 2 + [sem((n,))] * 6 + [sem((chips,))] * 4 + [sem((n,))] * 2 + [sem((m,))] * 2,
+        compiler_params=pltpu.CompilerParams(
+            collective_id=0, has_side_effects=True, vmem_limit_bytes=56 * 2**20
+        ),
+    )(
+        grad_out.T, residual, confounders, gram_factor, proj_weight,
+        doc_lengths.astype(F32)[:, None],
+    )
+
+
+def fits(n, m, grad_out, residual, confounders, gram_factor, proj_weight, doc_lengths):
+    docs, width = grad_out.shape
+    units, k = proj_weight.shape[0], gram_factor.shape[0]
+    whole = width % 128 == 0 and docs % (16 * m) == 0 and units % 16 == 0 and width % (16 * n) == 0
+    return whole and n % 2 == 0 and k >= 128 and k & (k - 1) == 0 and units * n == width * m and n <= 8
+
+
 def solution(mesh):
     placed = (P("dp", "col"), P("dp", "col"), P("dp", None), P(), P("dp", "col"), P(("dp", "col")))
+    n, m = mesh.shape["dp"], mesh.shape["col"]
+
+    def local(*args):
+        return fused(n, m, *args) if fits(n, m, *args) else shards(*args)
+
     return jax.shard_map(
-        shards,
+        local,
         mesh=mesh,
         in_specs=placed,
         out_specs=(P(("dp", "col"), None), P("dp", "col")),

time: 275 us -> 130 us (0.47)
  waiting for transfers between devices: 170 us -> 0 us
  Pallas kernels: 0 us -> 122 us
  other arithmetic: 44.2 us -> 0.66 us
  matrix products: 29.1 us -> 0 us
  between operations: 14 us -> 0.65 us
  local copies, waits for them, and re-layouts: 12 us -> 6.15 us
  starting transfers between devices: 5.08 us -> 0 us
    pallas_call x0 -> x1, Pallas kernels: none -> 122 us  [fused(): pl.pallas_call(functools.partial(kernel, n, m, (docs * n) ** (-0.5)), out...]
    all_gather x2 -> x0, waiting for transfers between devices: 92 us -> none  [the longest x1 46.8 us: shards(): lax.all_gather(proj_weight, 'dp', axis=0, tiled=True)]
    reduce_scatter x1 -> x0, waiting for transfers between devices: 53.7 us -> none  [shards(): lax.psum_scatter(lax.dot_general(grad_block, residual, (((0,), (0,)), (()...]
    another operation x3 -> x0, other arithmetic: 40.4 us -> none  [solve_gram(): lax.linalg.triangular_solve(factor, inner, left_side=True, lower=True, tr...]
    all_to_all x1 -> x0, waiting for transfers between devices: 21.8 us -> none  [shards(): lax.all_to_all(pooled, 'col', split_axis=0, concat_axis=1, tiled=True)]
    dot_general x4 -> x0, matrix products: 15.2 us -> none  [the longest x1 6.7 us: shards(): lax.dot_general(grad_block, residual, (((0,), (0,)), ((), ())), preferred...]
    another operation x14 -> x0, matrix products: 13.9 us -> none  [the longest x7 9.51 us: solve_gram(): inner = lax.linalg.triangular_solve(factor, rhs, left_side=True, lower=True)]
    another operation x13 -> x0, local copies, waits for them, and re-layouts: 10.7 us -> none
  transfers between devices with their start and end apart: 5 -> 0, of which waited for: 5 -> 0; matrix products, arithmetic and copies ran while one was open for 27% -> 0% of each run, Pallas kernels for 0% -> 0%
where the time goes in v1:
time: 130 us
  Pallas kernels  122 us (94%)
  local copies, waits for them, and re-layouts  6.15 us (5%)
    pallas_call x1, Pallas kernels, fused(): pl.pallas_call(functools.partial(kernel, n, m, (docs * n) ** (-0.5)), out...  122 us
    unnamed x5, local copies, waits for them, and re-layouts  5.44 us

profile of v1, /device:TPU:0, one launch (start us, length us, event | category | flops | bytes accessed | tf_op | source)
XLA Modules:
  0.0 129.8 jit_solution(14809366176809265549)
XLA Ops:
  0.6 0.7 convert_bitcast_fusion
  1.3 0.7 copy.9.len_ref
  2.0 2.0 %copy.8 = bf16[256,896]{0,1:T(8,128)(2,1)} copy(bf16[256,896]{1,0:T(8,128)(2,1)} %param.6) | data formatting | bytes 917504 | tf_op args[0]
  4.0 122.3 %shard_map.77 = (f32[64,3584]{1,0:T(8,128)}, f32[448,896]{1,0:T(8,128)}) custom-call(bf16[896,256]{1,0:T(8,128)(2,1)} %bitcast.3, bf16[256,896]{1,0:T(8,128)(2,1)} %res_ref.1, bf16[256,512]{1,0:T(8,128)(2,1)} %conf_ref.1, f32[512,512]{1,0:T(8,128)} %fac_ref.1, bf16[448,896]{1,0:T(8,128)(2,1)} %w_ref.1, f32[64,1]{1,0:T(8,128)} %copy.9.len_ref), custom_call_target="tpu_custom_call" | custom-call | tf_op jit(solution)/shard_map/pallas_call | solution.py:288
  126.3 0.0 copy-start
  126.3 2.3 %copy.12 = f32[64,3584]{1,0:T(8,128)} copy(f32[64,3584]{1,0:T(8,128)} %get-tuple-element.4) | data formatting | bytes 1835008
  128.6 0.0 copy-done
  128.6 1.2 copy.13
Async XLA Ops:
  126.3 2.3 %copy-start = (f32[448,896]{1,0:T(8,128)S(1)}, f32[448,896]{1,0:T(8,128)}, u32[]{:S(2)}) copy-start(f32[448,896]{1,0:T(8,128)} %get-tuple-element.5) | copy-start | bytes 4816900

commit v2 on v1

--- a/solution.py
+++ b/solution.py
@@ -59,7 +59,7 @@
     return dot(a, b, da, db, EXACT)
 
 
-def invert_factor(l_ref, inv_ref):
+def invert_factor(l_ref, inv_ref, between):
     k, base = l_ref.shape[0], 128
     r = lax.broadcasted_iota(jnp.int32, (base, base), 0)
     c = lax.broadcasted_iota(jnp.int32, (base, base), 1)
@@ -76,6 +76,7 @@
     for at, x in enumerate(parts):
         o = at * base
         inv_ref[o : o + base, o : o + base] = x
+    between()
     while size < k:
         for o in range(0, k, 2 * size):
             mid, end = o + size, o + 2 * size
@@ -85,11 +86,11 @@
 
 
 def kernel(
-    n, m, scale,
-    gt_ref, res_ref, conf_ref, fac_ref, w_ref, len_ref,
+    n, m,
+    gt_ref, res_ref, conf_ref, fac_ref, w_ref,
     tok_ref, dw_ref,
     gf, wf, rf, gx, r32, rb, mt, msib, mpre, mrecv, inv, cf, pb, prow, own,
-    g_s, g_r, w_s, w_r, r_s, r_r, x_s, x_r, a_s, a_r, m_s, m_r, c_s, c_r, p_s, p_r,
+    g_s, g_r, h_s, h_r, w_s, w_r, r_s, r_r, x_s, x_r, a_s, a_r, m_s, m_r, c_s, c_r, p_s, p_r,
 ):
     dp, col = lax.axis_index("dp"), lax.axis_index("col")
     core, chip = dp % 2, dp // 2
@@ -113,18 +114,21 @@
     def same_core(step):
         return lax.rem(chip + step, chips) * 2 + core
 
+    def chip_at(bx, by):
+        return lax.rem(chip // 2 + by, 2) * 2 + lax.rem(chip + bx, 2)
+
     def slot_of(t):
-        back = lax.rem(t, chips)
-        at = lax.rem(chip + chips - back, chips) * 2
-        return at + lax.rem(core + t // chips, 2)
+        at_core = lax.rem(core + t // chips, 2)
+        one, two = lax.rem(t, 2), lax.rem(t, chips) // 2
+        bx = (1 - at_core) * one + at_core * two
+        by = at_core * one + (1 - at_core) * two
+        return chip_at(bx, by) * 2 + at_core
+
+    side_a, side_b = chip_at(1 - core, core) * 2 + core, chip_at(core, 1 - core) * 2 + core
 
     def gather_start(ref, full, ss, rr):
-        copies = [
-            to_dp(ref, full.at[dp], ss.at[k], rr.at[k], same_core(k)) for k in range(1, chips)
-        ]
-        copies.append(to_dp(ref, full.at[dp], ss.at[chips], rr.at[chips], sib))
-        for copy in copies:
-            copy.start()
+        for k, d in ((1, side_a), (2, side_b), (chips, sib)):
+            to_dp(ref, full.at[dp], ss.at[k], rr.at[k], d).start()
         full[dp] = ref[...]
 
     def gather_wait(full, ss, rr, t):
@@ -133,6 +137,8 @@
 
     def gather_pass(full, ss, rr, t):
         at = full.at[slot_of(t)]
+        if t == 1:
+            to_dp(at, at, ss.at[3], rr.at[3], side_b).start()
         to_dp(at, at, ss.at[chips + t], rr.at[chips + t], sib).start()
 
     def gather_end(ref, full, ss, rr):
@@ -150,19 +156,55 @@
         )
     pl.semaphore_wait(barrier, n + m - 2)
 
-    mine = pl.ds(pl.multiple_of(col * width, width), width)
-    g_copies = [
-        to_col(gt_ref, gf.at[mine], g_s.at[k], g_r.at[k], lax.rem(col + k, m)) for k in range(1, m)
-    ]
-    for copy in g_copies:
-        copy.start()
+    def shard_at(c):
+        return gf.at[pl.ds(pl.multiple_of(c * width, width), width)]
+
+    def right(s):
+        at = shard_at(lax.max(col - (s - 1), 0))
+        return to_col(at, at, g_s.at[s], g_r.at[s], lax.rem(col + 1, m))
+
+    def left(s):
+        at = shard_at(lax.min(col + (s - 1), m - 1))
+        return to_col(at, at, h_s.at[s], h_r.at[s], lax.rem(col + m - 1, m))
+
+    def line_send(s, act):
+        @pl.when((col >= s - 1) & (col + 1 < m))
+        def _():
+            act(right(s))
+
+        @pl.when((col + s - 1 < m) & (col >= 1))
+        def _():
+            act(left(s))
+
+    def line_wait(s):
+        @pl.when(col >= s)
+        def _():
+            right(s).wait_recv()
+
+        @pl.when(col + s < m)
+        def _():
+            left(s).wait_recv()
+
+    gf[pl.ds(pl.multiple_of(col * width, width), width), :] = gt_ref[...]
+    line_send(1, lambda copy: copy.start())
     gather_start(w_ref, wf, w_s, w_r)
-    gf[mine, :] = gt_ref[...]
-
-    invert_factor(fac_ref, inv)
-
-    for copy in g_copies:
-        copy.wait_recv()
+
+    def line_next():
+        line_wait(1)
+        line_send(2, lambda copy: copy.start())
+
+    invert_factor(fac_ref, inv, line_next)
+
+    for t in (1, 2):
+        gather_wait(wf, w_s, w_r, t)
+        gather_pass(wf, w_s, w_r, t)
+    for s in range(2, m - 1):
+        line_wait(s)
+        line_send(s + 1, lambda copy: copy.start())
+    gather_wait(wf, w_s, w_r, 3)
+    gather_pass(wf, w_s, w_r, 3)
+    gather_start(res_ref, rf, r_s, r_r)
+    line_wait(m - 1)
 
     def add_units(t, first=False):
         at = slot_of(t)
@@ -174,8 +216,6 @@
 
     @pl.loop(1, chips)
     def _(t):
-        gather_wait(wf, w_s, w_r, t)
-        gather_pass(wf, w_s, w_r, t)
         add_units(t)
 
     @pl.loop(chips, n)
@@ -204,7 +244,6 @@
     for copy in m_copies:
         copy.start()
 
-    gather_start(res_ref, rf, r_s, r_r)
     x_copies = []
     for k in range(1, n):
         d = lax.rem(dp + k, n)
@@ -214,6 +253,9 @@
         copy.start()
     gx[dp] = gf[pl.ds(pl.multiple_of(dp * units, units), units), :]
 
+    for t in (1, 2):
+        gather_wait(rf, r_s, r_r, t)
+        gather_pass(rf, r_s, r_r, t)
     for copy in m_copies:
         copy.wait_recv()
     total = mpre[chip]
@@ -223,8 +265,7 @@
     own[...] = coef.astype(BF16)
     gather_start(own, cf, c_s, c_r)
 
-    @pl.loop(1, chips)
-    def _(t):
+    for t in range(1, chips):
         gather_wait(cf, c_s, c_r, t)
         gather_pass(cf, c_s, c_r, t)
 
@@ -245,13 +286,11 @@
 
     def add_docs(t, first=False):
         at = slot_of(t)
-        part = dot(gx[at], rf[at]) * scale
+        part = dot(gx[at], rf[at])
         dw_ref[...] = part if first else dw_ref[...] + part
 
-    @pl.loop(1, chips)
-    def _(t):
-        gather_wait(rf, r_s, r_r, t)
-        gather_pass(rf, r_s, r_r, t)
+    gather_wait(rf, r_s, r_r, 3)
+    gather_pass(rf, r_s, r_r, 3)
 
     add_docs(0, True)
     for copy in x_copies:
@@ -270,12 +309,14 @@
         copy.wait_recv()
     prow[col] = pb[pl.ds(pl.multiple_of(col * share, share), share), :]
     for c in range(m):
-        tok_ref[:, c * width : (c + 1) * width] = prow[c].astype(F32) / len_ref[...]
+        tok_ref[:, c * width : (c + 1) * width] = prow[c]
 
     gather_end(w_ref, wf, w_s, w_r)
     gather_end(res_ref, rf, r_s, r_r)
     gather_end(own, cf, c_s, c_r)
-    for copy in g_copies + a_copies + m_copies + x_copies + p_copies:
+    for s in range(1, m):
+        line_send(s, lambda copy: copy.wait_send())
+    for copy in a_copies + m_copies + x_copies + p_copies:
         copy.wait_send()
 
 
@@ -285,13 +326,13 @@
     share, rows, chips = docs // m, width // n, n // 2
     sem = pltpu.SemaphoreType.DMA
     vmem = pl.BlockSpec(memory_space=pltpu.VMEM)
-    return pl.pallas_call(
-        functools.partial(kernel, n, m, (docs * n) ** (-0.5)),
+    rows_out, total = pl.pallas_call(
+        functools.partial(kernel, n, m),
         out_shape=(
-            jax.ShapeDtypeStruct((share, width * m), F32),
+            jax.ShapeDtypeStruct((share, width * m), BF16),
             jax.ShapeDtypeStruct((units, width), F32),
         ),
-        in_specs=[vmem] * 6,
+        in_specs=[vmem] * 5,
         out_specs=(vmem, vmem),
         scratch_shapes=[
             pltpu.VMEM((width * m, docs), BF16),
@@ -310,21 +351,19 @@
             pltpu.VMEM((m, share, width), BF16),
             pltpu.VMEM((rows, k), BF16),
         ]
-        + [sem((m,))] * 2 + [sem((n,))] * 6 + [sem((chips,))] * 4 + [sem((n,))] * 2 + [sem((m,))] * 2,
+        + [sem((m,))] * 4 + [sem((n,))] * 6 + [sem((chips,))] * 4 + [sem((n,))] * 2 + [sem((m,))] * 2,
         compiler_params=pltpu.CompilerParams(
             collective_id=0, has_side_effects=True, vmem_limit_bytes=56 * 2**20
         ),
-    )(
-        grad_out.T, residual, confounders, gram_factor, proj_weight,
-        doc_lengths.astype(F32)[:, None],
-    )
+    )(grad_out.T, residual, confounders, gram_factor, proj_weight)
+    return rows_out.astype(F32) / doc_lengths.astype(F32)[:, None], total * (docs * n) ** (-0.5)
 
 
 def fits(n, m, grad_out, residual, confounders, gram_factor, proj_weight, doc_lengths):
     docs, width = grad_out.shape
     units, k = proj_weight.shape[0], gram_factor.shape[0]
     whole = width % 128 == 0 and docs % (16 * m) == 0 and units % 16 == 0 and width % (16 * n) == 0
-    return whole and n % 2 == 0 and k >= 128 and k & (k - 1) == 0 and units * n == width * m and n <= 8
+    return whole and n == 8 and m > 2 and k >= 128 and k & (k - 1) == 0 and units * n == width * m
 
 
 def solution(mesh):

time: 130 us -> 106 us (0.82)
  Pallas kernels: 122 us -> 99.7 us
  local copies, waits for them, and re-layouts: 6.15 us -> 2 us
  other arithmetic: 0.66 us -> 3.83 us
    pallas_call x1, Pallas kernels: 122 us -> 99.7 us  [fused(): pl.pallas_call(functools.partial(kernel, n, m), out_shape=(jax.ShapeDtype...]
    unnamed x5, local copies, waits for them, and re-layouts: 5.44 us -> 2 us
    mul x0 -> x1, other arithmetic: none -> 2.77 us  [fused(): total * (docs * n) ** (-0.5)]
where the time goes in v2:
time: 106 us
  Pallas kernels  99.7 us (94%)
  other arithmetic  3.83 us (4%)
  local copies, waits for them, and re-layouts  2 us (2%)
    pallas_call x1, Pallas kernels, fused(): pl.pallas_call(functools.partial(kernel, n, m), out_shape=(jax.ShapeDtype...  99.7 us
    mul x1, other arithmetic, fused(): total * (docs * n) ** (-0.5)  2.77 us

profile of v2, /device:TPU:0, one launch (start us, length us, event | category | flops | bytes accessed | tf_op | source)
XLA Modules:
  0.0 106.2 jit_solution(16521012841274512726)
XLA Ops:
  0.6 2.0 %copy.8 = bf16[256,896]{0,1:T(8,128)(2,1)} copy(bf16[256,896]{1,0:T(8,128)(2,1)} %param.6) | data formatting | bytes 917504 | tf_op args[0]
  2.6 99.7 %shard_map.77 = (bf16[64,3584]{1,0:T(8,128)(2,1)}, f32[448,896]{1,0:T(8,128)}) custom-call(bf16[896,256]{1,0:T(8,128)(2,1)} %bitcast.1, bf16[256,896]{1,0:T(8,128)(2,1)} %res_ref.1, bf16[256,512]{1,0:T(8,128)(2,1)} %conf_ref.1, f32[512,512]{1,0:T(8,128)} %fac_ref.1, bf16[448,896]{1,0:T(8,128)(2,1)} %w_ref.1), custom_call_target="tpu_custom_call" | custom-call | tf_op jit(solution)/shard_map/pallas_call | solution.py:329
  102.4 0.0 copy-start.1
  102.4 0.0 copy-start
  102.4 2.8 %broadcast_multiply_fusion = f32[448,896]{1,0:T(8,128)} fusion(f32[448,896]{1,0:T(8,128)} %get-tuple-element.5), kind=kLoop, calls=%fused_computation.1 | loop fusion | flops 401408 | bytes 3211264 | tf_op jit(solution)/shard_map/mul | solution.py:359
  105.2 0.0 copy-done.1
  105.2 0.0 copy-done
  105.2 1.1 convert_divide_fusion
  (1 shorter events, 0.0 us)
Async XLA Ops:
  102.4 2.8 %copy-start.1 = (s32[64]{0:T(128)S(1)}, s32[64]{0:T(128)}, u32[]{:S(2)}) copy-start(s32[64]{0:T(128)} %param.11) | copy-start | bytes 772
  102.4 2.8 %copy-start = (bf16[64,3584]{1,0:T(8,128)(2,1)S(1)}, bf16[64,3584]{1,0:T(8,128)(2,1)}, u32[]{:S(2)}) copy-start(bf16[64,3584]{1,0:T(8,128)(2,1)} %get-tuple-element.4) | copy-start | bytes 1376260

commit v3 on v2

--- a/solution.py
+++ b/solution.py
@@ -244,15 +244,6 @@
     for copy in m_copies:
         copy.start()
 
-    x_copies = []
-    for k in range(1, n):
-        d = lax.rem(dp + k, n)
-        piece = gf.at[pl.ds(pl.multiple_of(d * units, units), units)]
-        x_copies.append(to_dp(piece, gx.at[dp], x_s.at[k], x_r.at[k], d))
-    for copy in x_copies:
-        copy.start()
-    gx[dp] = gf[pl.ds(pl.multiple_of(dp * units, units), units), :]
-
     for t in (1, 2):
         gather_wait(rf, r_s, r_r, t)
         gather_pass(rf, r_s, r_r, t)
@@ -264,6 +255,15 @@
     coef = exact(exact(total, inv[...], 1, 1), inv[...])
     own[...] = coef.astype(BF16)
     gather_start(own, cf, c_s, c_r)
+    x_copies = []
+    for k in range(1, n):
+        d = lax.rem(dp + k, n)
+        piece = gf.at[pl.ds(pl.multiple_of(d * units, units), units)]
+        x_copies.append(to_dp(piece, gx.at[dp], x_s.at[k], x_r.at[k], d))
+    for copy in x_copies:
+        copy.start()
+    gx[dp] = gf[pl.ds(pl.multiple_of(dp * units, units), units), :]
+
 
     for t in range(1, chips):
         gather_wait(cf, c_s, c_r, t)
@@ -286,6 +286,9 @@
 
     def add_docs(t, first=False):
         at = slot_of(t)
+        if not first:
+            k = lax.rem(dp + n - at, n)
+            to_dp(gx.at[at], gx.at[at], x_s.at[k], x_r.at[k], sib).wait_recv()
         part = dot(gx[at], rf[at])
         dw_ref[...] = part if first else dw_ref[...] + part
 
@@ -293,8 +296,6 @@
     gather_pass(rf, r_s, r_r, 3)
 
     add_docs(0, True)
-    for copy in x_copies:
-        copy.wait_recv()
 
     @pl.loop(1, chips)
     def _(t):

time: 106 us -> 106 us (level)
  no operation moved by 1% of the time
where the time goes in v3:
time: 106 us
  Pallas kernels  99.3 us (94%)
  other arithmetic  3.83 us (4%)
  local copies, waits for them, and re-layouts  2 us (2%)
    pallas_call x1, Pallas kernels, fused(): pl.pallas_call(functools.partial(kernel, n, m), out_shape=(jax.ShapeDtype...  99.3 us
    mul x1, other arithmetic, fused(): total * (docs * n) ** (-0.5)  2.77 us

profile of v3, /device:TPU:0, one launch (start us, length us, event | category | flops | bytes accessed | tf_op | source)
XLA Modules:
  0.0 105.8 jit_solution(10429438504323382262)
XLA Ops:
  0.6 2.0 %copy.8 = bf16[256,896]{0,1:T(8,128)(2,1)} copy(bf16[256,896]{1,0:T(8,128)(2,1)} %param.6) | data formatting | bytes 917504 | tf_op args[0]
  2.6 99.3 %shard_map.77 = (bf16[64,3584]{1,0:T(8,128)(2,1)}, f32[448,896]{1,0:T(8,128)}) custom-call(bf16[896,256]{1,0:T(8,128)(2,1)} %bitcast.1, bf16[256,896]{1,0:T(8,128)(2,1)} %res_ref.1, bf16[256,512]{1,0:T(8,128)(2,1)} %conf_ref.1, f32[512,512]{1,0:T(8,128)} %fac_ref.1, bf16[448,896]{1,0:T(8,128)(2,1)} %w_ref.1), custom_call_target="tpu_custom_call" | custom-call | tf_op jit(solution)/shard_map/pallas_call | solution.py:330
  102.0 0.0 copy-start.1
  102.0 0.0 copy-start
  102.0 2.8 %broadcast_multiply_fusion = f32[448,896]{1,0:T(8,128)} fusion(f32[448,896]{1,0:T(8,128)} %get-tuple-element.5), kind=kLoop, calls=%fused_computation.1 | loop fusion | flops 401408 | bytes 3211264 | tf_op jit(solution)/shard_map/mul | solution.py:360
  104.7 0.0 copy-done.1
  104.7 0.0 copy-done
  104.8 1.1 %convert_divide_fusion = f32[64,3584]{1,0:T(8,128)} fusion(bf16[64,3584]{1,0:T(8,128)(2,1)S(1)} %copy-done, f32[64]{0:T(128)S(1)} %convert_element_type.7), kind=kLoop, calls=%fused_computation | loop fusion | flops 458752 | bytes 1376512 | tf_op jit(solution)/shard_map/div | solution.py:360
  (1 shorter events, 0.0 us)
Async XLA Ops:
  102.0 2.8 %copy-start.1 = (s32[64]{0:T(128)S(1)}, s32[64]{0:T(128)}, u32[]{:S(2)}) copy-start(s32[64]{0:T(128)} %param.11) | copy-start | bytes 772
  102.0 2.8 %copy-start = (bf16[64,3584]{1,0:T(8,128)(2,1)S(1)}, bf16[64,3584]{1,0:T(8,128)(2,1)}, u32[]{:S(2)}) copy-start(bf16[64,3584]{1,0:T(8,128)(2,1)} %get-tuple-element.4) | copy-start | bytes 1376260
